TPU v7x, 512 devices: a whole 4x8x8 slice. The times are simulated.
512 devices in a mesh: dp: 8 (over x, core), tensor: 8 (over z), vocab: 8 (over y).
Axes of the slice: x: 4, y: 8, z: 8, core: 2. Of those that a mesh axis runs over, the one named last changes fastest.
Arguments:
- hidden_in: bfloat16 [1024, 4608], P('dp')
- norm_pre: float32 [4608], replicated, may hold values from 0.1 to 1.9
- w_gate: bfloat16 [4608, 18432], P('dp', ('tensor', 'vocab')), may hold values from -0.09375 to 0.09375
- w_up: bfloat16 [4608, 18432], P('dp', ('tensor', 'vocab')), may hold values from -0.09375 to 0.09375
- w_down: bfloat16 [18432, 4608], P(('tensor', 'vocab'), 'dp'), may hold values from -0.125 to 0.125
- norm_post: float32 [4608], replicated, may hold values from 0.1 to 1.9
- norm_final: float32 [4608], replicated, may hold values from 0.1 to 1.9
- unembed: bfloat16 [4608, 131072], P(None, ('dp', 'tensor', 'vocab')), may hold values from -0.375 to 0.375
- token_ids: int32 [1024], P('dp'), may hold values from 0 to 131071
- lengths: int32 [16], P('dp'), may hold values from 1 to 63, as said below
Outputs:
- token_logprob: float32 [1024], P('dp')
Inputs may be any that keep to these rules, and one draw needn't show every extreme that they name: The rollouts are numbered by index of dp, 2 to each; the lengths of the rollouts of one index of dp sum to at most 64, and to exactly 64 on at least one index of dp, whose rollouts have lengths 64 - 1 and 1.
All inputs are finite; a program needn't handle non-finite values.
Results may differ from a plain program's by a relative error of at most 0.0035.
Values may be sent and summed in bfloat16 or wider, within the bound.
A program may use at most 64 MiB of HBM per device.

v0:
```python
import jax
import jax.numpy as jnp
from jax import lax
from jax.sharding import PartitionSpec as P

EPS = 1e-06
CAP = 30.0


def on_device(
    hidden_in, norm_pre, w_gate, w_up, w_down, norm_post, norm_final, unembed, token_ids, lengths
):
    slot_count = hidden_in.shape[0]
    segment = slot_count // lengths.shape[0]
    position = jnp.arange(slot_count, dtype=jnp.int32)
    which = (position // segment)[:, None] == jnp.arange(lengths.shape[0], dtype=jnp.int32)[None, :]
    bounds = jnp.sum(jnp.where(which, lengths[None, :], 0), axis=1)
    scored = position % segment < bounds
    stream_in = hidden_in.astype(jnp.float32)
    normed = (
        stream_in
        * lax.rsqrt(jnp.mean(stream_in * stream_in, axis=1, keepdims=True) + EPS)
        * norm_pre
    ).astype(jnp.bfloat16)
    spread = lax.all_to_all(normed, "dp", split_axis=1, concat_axis=0, tiled=True)
    paired = jnp.concatenate([w_gate, w_up], axis=1)
    gate_up = lax.psum_scatter(
        jnp.dot(spread, paired, preferred_element_type=jnp.float32).astype(jnp.bfloat16),
        "dp",
        scatter_dimension=0,
        tiled=True,
    ).astype(jnp.float32)
    units = w_gate.shape[1]
    hidden = (jax.nn.silu(gate_up[:, :units]) * gate_up[:, units:]).astype(jnp.bfloat16)
    branch = jnp.dot(
        hidden, lax.all_gather(w_down, "dp", axis=1, tiled=True), preferred_element_type=jnp.float32
    )
    summed = lax.psum(branch, ("tensor", "vocab"))
    stream = (
        stream_in
        + summed * lax.rsqrt(jnp.mean(summed * summed, axis=1, keepdims=True) + EPS) * norm_post
    )
    final = (
        stream * lax.rsqrt(jnp.mean(stream * stream, axis=1, keepdims=True) + EPS) * norm_final
    ).astype(jnp.bfloat16)
    every_row, every_target = (
        lax.all_gather(final, "dp", axis=0, tiled=True),
        lax.all_gather(token_ids, "dp", axis=0, tiled=True),
    )
    shard = unembed.shape[1]
    offset = lax.axis_index(("dp", "tensor", "vocab")) * shard
    capped = CAP * jnp.tanh(jnp.dot(every_row, unembed, preferred_element_type=jnp.float32) / CAP)
    totals = jnp.sum(jnp.exp(capped - CAP), axis=1)
    matches = jnp.arange(shard, dtype=jnp.int32)[None, :] + offset == every_target[:, None]
    sampled = jnp.sum(jnp.where(matches, capped, 0.0), axis=1)
    every_total, every_sampled = lax.psum((totals, sampled), ("dp", "tensor", "vocab"))
    count = every_total.shape[0] // lax.axis_size("dp")
    start = lax.axis_index("dp") * count
    own_total = lax.dynamic_slice_in_dim(every_total, start, count, 0)
    own_target = lax.dynamic_slice_in_dim(every_sampled, start, count, 0)
    logprob = own_target - CAP - jnp.log(own_total)
    return jnp.where(scored, logprob, 0.0)


def solution(mesh):
    in_specs = (
        P("dp", None),
        P(),
        P("dp", ("tensor", "vocab")),
        P("dp", ("tensor", "vocab")),
        P(("tensor", "vocab"), "dp"),
        P(),
        P(),
        P(None, ("dp", "tensor", "vocab")),
        P("dp"),
        P("dp"),
    )
    out_specs = P("dp")
    return jax.shard_map(
        on_device, mesh=mesh, in_specs=in_specs, out_specs=out_specs, check_vma=False
    )
```

profile of v0, /device:TPU:1, one launch (start us, length us, event | category | flops | bytes accessed | tf_op | source)
XLA Modules:
  0.0 464.3 jit_solution(11924387753720224544)
XLA Ops:
  6.5 0.0 copy-start
  6.5 0.0 reduce-scatter.4.cloned.1.call-start
  6.5 1.7 fusion
  8.3 2.6 fusion.2
  10.9 1.7 copy.17
  12.6 0.0 copy-start.6
  12.6 0.0 copy-start.7
  12.6 26.1 %all_to_all.19 = bf16[128,8,576]{0,2,1:T(8,128)(2,1)S(1)} all-to-all(bf16[128,8,576]{0,2,1:T(8,128)(2,1)S(1)} %bitcast.20), channel_id=1, replica_groups=mesh['dp'=8,'tensor'=8,'vocab'=8] {'dp'}, dimensions={1} | all-to-all | bytes 2359296 | tf_op jit(solution)/shard_map/all_to_all | solution.py:25
  38.7 0.0 copy-done.6
  38.7 0.0 copy-done.7
  38.7 1.1 convolution_convert_fusion
  39.8 1.4 copy.20
  41.2 0.0 reduce-scatter.4.cloned.1.call-update
  41.3 0.0 all-gather.7.cloned.1.call-start
  41.3 0.7 all-gather.7.cloned.1.call-update
  42.0 0.0 all-reduce.3.cloned.1.call-start
  42.1 34.6 %reduce-scatter.4.cloned.1.call-done = bf16[128,576]{1,0:T(8,128)(2,1)} async-done(((bf16[1024,576]{1,0:T(8,128)(2,1)}), bf16[128,576]{1,0:T(8,128)(2,1)}) %reduce-scatter.4.cloned.1.call-update) | async-done | bytes 147472
  76.6 1.1 copy.21
  77.7 34.4 %all-gather.7.cloned.1.call-done = bf16[8,576,288]{1,2,0:T(8,128)(2,1)} async-done(((bf16[1,576,288]{1,2,0:T(8,128)(2,1)}), bf16[8,576,288]{1,2,0:T(8,128)(2,1)}) %all-gather.7.cloned.1.call-update) | async-done | bytes 2654224 | tf_op jit(solution)/shard_map/all_gather | solution.py:36
  112.1 4.5 copy.19
  116.5 5.6 %reshape.53 = bf16[4608,288]{0,1:T(8,128)(2,1)} reshape(bf16[8,576,288]{1,0,2:T(8,128)(2,1)} %copy.19) | data formatting | bytes 5308416
  122.1 4.0 fusion.11
  126.1 0.0 copy-start.2
  126.1 0.0 all-reduce.3.cloned.1.call-update
  126.1 0.0 all-gather.5.cloned.1.call-start
  126.2 160.6 %all-reduce.3.cloned.1.call-done = f32[128,4608]{1,0:T(8,128)} async-done(((f32[128,4608]{1,0:T(8,128)}), f32[128,4608]{1,0:T(8,128)}) %all-reduce.3.cloned.1.call-update) | async-done | bytes 2359312 | tf_op jit(solution)/shard_map/psum | solution.py:38
  286.8 0.0 copy-start.1
  286.8 2.1 multiply_reduce_fusion.1
  288.9 0.0 copy-start.3
  288.9 0.0 copy-start.4
  288.9 0.0 copy-done.2
  288.9 0.3 copy-done.1
  289.2 1.4 multiply_reduce_fusion
  290.6 0.0 copy-done.3
  290.6 0.0 copy-done.4
  290.6 0.0 copy-start.5
  290.6 0.0 copy-start.8
  290.6 1.6 multiply_convert_fusion
  292.2 0.0 all-gather.5.cloned.1.call-update
  292.2 0.0 copy-done.5
  292.3 14.7 %all-gather = s32[8,1,128]{2,1,0:T(1,128)S(1)} all-gather(s32[1,1,128]{2,1,0:T(1,128)S(1)} %bitcast.23), channel_id=1, replica_groups=mesh['dp'=8,'tensor'=8,'vocab'=8] {'dp'}, dimensions={0}, use_global_device_ids=true | all-gather | bytes 4608 | tf_op jit(solution)/shard_map/all_gather | solution.py:48
  307.0 0.0 copy-done.8
  307.0 0.1 fusion.14
  307.0 45.5 %all-gather.5.cloned.1.call-done = bf16[1024,4608]{1,0:T(8,128)(2,1)} async-done(((bf16[128,4608]{1,0:T(8,128)(2,1)}), bf16[1024,4608]{1,0:T(8,128)(2,1)}) %all-gather.5.cloned.1.call-update) | async-done | bytes 9437200 | tf_op jit(solution)/shard_map/all_gather | solution.py:47
  352.5 0.0 copy-done
  352.5 6.6 %select_reduce_fusion = (f32[1024]{0:T(1024)S(1)}, f32[1024]{0:T(1024)S(1)}) fusion(s32[1024]{0:T(1024)S(1)} %bitcast.22, s32[256]{0:T(256)S(1)} %iota_add_fusion, bf16[1024,4608]{1,0:T(8,128)(2,1)} %all-gather.5.cloned.1.call-done, bf16[4608,256]{1,0:T(8,128)(2,1)S(1)} %copy-done), kind=kOutput, calls=%fused_computation.16 | convolution fusion | flops 2417752064 | bytes 11809792 | tf_op jit(solution)/shard_map/dot_general | solution.py:52
  359.1 98.1 %all-reduce = (f32[1024]{0:T(1024)S(1)}, f32[1024]{0:T(1024)S(1)}) all-reduce(f32[1024]{0:T(1024)S(1)} %get-tuple-element.6, f32[1024]{0:T(1024)S(1)} %get-tuple-element.5), channel_id=1, replica_groups=mesh['dp'=8,'tensor'=8,'vocab'=8] {'dp','tensor','vocab'}, use_global_device_ids=true, to_apply=%region_9.10 | all-reduce | flops 2048 | bytes 16384 | tf_op jit(solution)/shard_map/psum | solution.py:56
  457.2 0.6 compare_select_fusion
  (6 shorter events, 0.1 us)
Async XLA Ops:
  6.5 346.0 %copy-start = (bf16[4608,256]{1,0:T(8,128)(2,1)S(1)}, bf16[4608,256]{1,0:T(8,128)(2,1)}, u32[]{:S(2)}) copy-start(bf16[4608,256]{1,0:T(8,128)(2,1)} %param.17) | copy-start | bytes 7077892
  6.5 70.1 %reduce-scatter.4.cloned.1.call-start = ((), (), s32[]{:S(2)}) async-start(), calls=%async_computation.5 | async-start | bytes 1474560
  12.6 26.1 %copy-start.6 = (bf16[576,288]{0,1:T(8,128)(2,1)S(1)}, bf16[576,288]{0,1:T(8,128)(2,1)}, u32[]{:S(2)}) copy-start(bf16[576,288]{0,1:T(8,128)(2,1)} %param.13) | copy-start | bytes 995332
  12.6 26.1 %copy-start.7 = (bf16[576,288]{0,1:T(8,128)(2,1)S(1)}, bf16[576,288]{0,1:T(8,128)(2,1)}, u32[]{:S(2)}) copy-start(bf16[576,288]{0,1:T(8,128)(2,1)} %param.12) | copy-start | bytes 995332
  41.3 70.8 %all-gather.7.cloned.1.call-start = ((), (), s32[]{:S(2)}) async-start(), calls=%async_computation.4 | async-start | bytes 3317760 | tf_op jit(solution)/shard_map/all_gather | solution.py:36
  42.0 244.8 %all-reduce.3.cloned.1.call-start = ((), (), s32[]{:S(2)}) async-start(), calls=%async_computation.2 | async-start | bytes 4718592 | tf_op jit(solution)/shard_map/psum | solution.py:38
  126.1 162.8 %copy-start.2 = (bf16[128,4608]{1,0:T(8,128)(2,1)S(1)}, bf16[128,4608]{1,0:T(8,128)(2,1)}, u32[]{:S(2)}) copy-start(bf16[128,4608]{1,0:T(8,128)(2,1)} %param.10) | copy-start | bytes 3538948
  126.1 226.4 %all-gather.5.cloned.1.call-start = ((), (), s32[]{:S(2)}) async-start(), calls=%async_computation.3 | async-start | bytes 10616832 | tf_op jit(solution)/shard_map/all_gather | solution.py:47
  286.8 2.4 copy-start.1
  288.9 1.7 copy-start.3
  288.9 1.7 copy-start.4
  290.6 1.7 copy-start.5
  290.6 16.4 %copy-start.8 = (s32[2]{0:T(128)S(1)}, s32[2]{0:T(128)}, u32[]{:S(2)}) copy-start(s32[2]{0:T(128)} %param.19) | copy-start | bytes 28
Sparse Core Ops, SparseCore 0:
  41.4 35.1 reduce-scatter.3
  78.7 33.2 all-gather.6
  126.3 160.4 all-reduce.2
  292.4 60.1 all-gather.4
where the time goes:
time: 465 us; the launch traced here: 464 us
  waiting for transfers between devices  276 us (59%)
  blocking collectives  139 us (30%)
  local copies, waits for them, and re-layouts  14.6 us (3%)
  between operations  13.3 us (3%)
  matrix products  11.7 us (3%)
  other arithmetic  10.1 us (2%)
    psum x1, waiting for transfers between devices, on_device(): summed = lax.psum(branch, ('tensor', 'vocab'))  161 us
    psum x1, blocking collectives, on_device(): lax.psum((totals, sampled), ('dp', 'tensor', 'vocab'))  98.1 us
    all_gather x1, waiting for transfers between devices, on_device(): lax.all_gather(final, 'dp', axis=0, tiled=True)  45.5 us
    unnamed x5, waiting for transfers between devices  35.3 us
    all_gather x1, waiting for transfers between devices, on_device(): lax.all_gather(w_down, 'dp', axis=1, tiled=True)  34.4 us
    all_to_all x1, blocking collectives, on_device(): lax.all_to_all(normed, 'dp', split_axis=1, concat_axis=0, tiled=True)  26.1 us
    all_gather x1, blocking collectives, on_device(): lax.all_gather(token_ids, 'dp', axis=0, tiled=True)  14.7 us
  transfers between devices with their start and end apart: 4, of which 4 were waited for; matrix products, arithmetic and copies ran while one was open for 0% of the time, Pallas kernels for 0%

commit v1 on v0

--- a/solution.py
+++ b/solution.py
@@ -5,6 +5,12 @@
 
 EPS = 1e-06
 CAP = 30.0
+
+
+def chunk_step_on(obj, axis_k):
+    obj = jnp.moveaxis(obj, 0, axis_k)
+    v_next = obj.shape
+    return obj.reshape(*v_next[:axis_k], v_next[axis_k] * v_next[axis_k + 1], *v_next[axis_k + 2 :])
 
 
 def on_device(
@@ -32,9 +38,25 @@
     ).astype(jnp.float32)
     units = w_gate.shape[1]
     hidden = (jax.nn.silu(gate_up[:, :units]) * gate_up[:, units:]).astype(jnp.bfloat16)
-    branch = jnp.dot(
-        hidden, lax.all_gather(w_down, "dp", axis=1, tiled=True), preferred_element_type=jnp.float32
-    )
+
+    def post_sections(axis_name, local_block, dim_i):
+        extent = jax.lax.axis_size(axis_name)
+        by_rank = [(d, (d + 1) % extent) for d in range(extent)]
+        runs = [(it, j0) for j0, it in by_rank]
+        big, item_now = ([], [])
+        for q in range(extent - 1):
+            if q % 2 == 0:
+                big.append(jax.lax.ppermute(big[-1] if big else local_block, axis_name, by_rank))
+            else:
+                item_now.append(
+                    jax.lax.ppermute(item_now[-1] if item_now else local_block, axis_name, runs)
+                )
+        piece_next = jnp.stack([*big[::-1], local_block, *item_now], axis=0)
+        s_next = jax.lax.axis_index(axis_name) - len(big)
+        piece_next = piece_next[(jnp.arange(extent) - s_next) % extent]
+        return chunk_step_on(piece_next, dim_i)
+
+    branch = jnp.dot(hidden, post_sections("dp", w_down, 1), preferred_element_type=jnp.float32)
     summed = lax.psum(branch, ("tensor", "vocab"))
     stream = (
         stream_in

time: 465 us -> 437 us (0.940)
  waiting for transfers between devices: 276 us -> 233 us
  blocking collectives: 139 us -> 113 us
  starting transfers between devices: 0.12 us -> 24.3 us
  local copies, waits for them, and re-layouts: 14.6 us -> 29.9 us
    all_gather x1 -> x0, waiting for transfers between devices: 34.4 us -> none  [on_device(): lax.all_gather(w_down, 'dp', axis=1, tiled=True)]
    unnamed x5 -> x4, waiting for transfers between devices: 35.3 us -> 3.01 us
    all_to_all x1 -> x0, blocking collectives: 26.1 us -> none  [on_device(): lax.all_to_all(normed, 'dp', split_axis=1, concat_axis=0, tiled=True)]
    ppermute x0 -> x7, waiting for transfers between devices: none -> 23.7 us  [the longest x4 19 us: post_sections(): jax.lax.ppermute(big[-1] if big else local_block, axis_name, by_rank)]
    ppermute x0 -> x7, starting transfers between devices: none -> 13.9 us  [the longest x3 7.31 us: post_sections(): jax.lax.ppermute(item_now[-1] if item_now else local_block, axis_name, runs)]
    all_to_all x0 -> x1, starting transfers between devices: none -> 10.3 us  [on_device(): lax.all_to_all(normed, 'dp', split_axis=1, concat_axis=0, tiled=True)]
    reshape x0 -> x1, local copies, waits for them, and re-layouts: none -> 5.63 us  [chunk_step_on(): obj.reshape(*v_next[:axis_k], v_next[axis_k] * v_next[axis_k + 1], *v_nex...]
    unnamed x21 -> x29, local copies, waits for them, and re-layouts: 8.42 us -> 13.2 us
  transfers between devices with their start and end apart: 4 -> 11, of which waited for: 4 -> 6; matrix products, arithmetic and copies ran while one was open for 0% -> 7% of each run, Pallas kernels for 0% -> 0%
where the time goes in v1:
time: 437 us; the launch traced here: 436 us
  waiting for transfers between devices  233 us (53%)
  blocking collectives  113 us (26%)
  local copies, waits for them, and re-layouts  29.9 us (7%)
  starting transfers between devices  24.3 us (6%)
  matrix products  13.8 us (3%)
  between operations  13.2 us (3%)
  other arithmetic  9.15 us (2%)
    psum x1, waiting for transfers between devices, on_device(): summed = lax.psum(branch, ('tensor', 'vocab'))  161 us
    psum x1, blocking collectives, on_device(): lax.psum((totals, sampled), ('dp', 'tensor', 'vocab'))  98.1 us
    all_gather x1, waiting for transfers between devices, on_device(): lax.all_gather(final, 'dp', axis=0, tiled=True)  45.5 us
    ppermute x4, waiting for transfers between devices, post_sections(): jax.lax.ppermute(big[-1] if big else local_block, axis_name, by_rank)  19 us
    all_gather x1, blocking collectives, on_device(): lax.all_gather(token_ids, 'dp', axis=0, tiled=True)  14.7 us
    unnamed x29, local copies, waits for them, and re-layouts  13.2 us
    all_to_all x1, starting transfers between devices, on_device(): lax.all_to_all(normed, 'dp', split_axis=1, concat_axis=0, tiled=True)  10.3 us
  transfers between devices with their start and end apart: 11, of which 6 were waited for; matrix products, arithmetic and copies ran while one was open for 7% of the time, Pallas kernels for 0%

profile of v1, /device:TPU:1, one launch (start us, length us, event | category | flops | bytes accessed | tf_op | source)
XLA Modules:
  0.0 436.2 jit_solution(18263665475051747251)
XLA Ops:
  6.5 1.7 fusion
  8.3 1.6 fusion.2
  9.9 1.4 copy.17
  11.3 10.3 %all-to-all-start = ((bf16[128,8,576]{0,2,1:T(8,128)(2,1)}), bf16[128,8,576]{0,2,1:T(8,128)(2,1)S(1)}, u32[]{:S(2)}, u32[]{:S(2)}) async-start(bf16[128,8,576]{0,2,1:T(8,128)(2,1)} %bitcast.2), calls=%async_computation | async-start | bytes 2359296 | tf_op jit(solution)/shard_map/all_to_all | solution.py:31
  21.7 1.6 collective-permute-start
  23.3 15.8 %collective-permute-done = bf16[288,576]{1,0:T(8,128)(2,1)S(1)} collective-permute-done((bf16[288,576]{1,0:T(8,128)(2,1)}, bf16[288,576]{1,0:T(8,128)(2,1)S(1)}, u32[]{:S(2)}, u32[]{:S(2)}) %collective-permute-start) | collective-permute-done | bytes 331808 | tf_op jit(solution)/shard_map/ppermute | solution.py:49
  39.1 2.4 collective-permute-start.1
  41.5 1.2 collective-permute-start.4
  42.7 3.2 collective-permute-done.1
  45.9 2.6 collective-permute-start.2
  48.5 3.2 convolution_convert_fusion
  51.7 2.4 copy.20
  54.2 0.0 reduce-scatter.4.cloned.1.call-update
  54.2 0.0 all-reduce.3.cloned.1.call-start
  54.2 2.5 collective-permute-start.5
  56.7 4.7 %collective-permute-done.5 = bf16[288,576]{1,0:T(8,128)(2,1)S(1)} collective-permute-done((bf16[288,576]{1,0:T(8,128)(2,1)}, bf16[288,576]{1,0:T(8,128)(2,1)S(1)}, u32[]{:S(2)}, u32[]{:S(2)}) %collective-permute-start.5) | collective-permute-done | bytes 331808 | tf_op jit(solution)/shard_map/ppermute | solution.py:52
  61.4 3.6 collective-permute-start.6
  65.0 1.8 bitcast_dynamic-update-slice_fusion.7
  66.8 1.8 bitcast_dynamic-update-slice_fusion.6
  68.5 1.8 bitcast_dynamic-update-slice_fusion.5
  70.3 0.8 bitcast_dynamic-update-slice_fusion.4
  71.1 0.8 bitcast_dynamic-update-slice_fusion.3
  71.9 1.8 bitcast_dynamic-update-slice_fusion.2
  73.6 0.8 bitcast_dynamic-update-slice_fusion.1
  74.4 0.8 bitcast_dynamic-update-slice_fusion
  75.2 4.4 %gather_fusion = bf16[8,288,576]{2,1,0:T(8,128)(2,1)} fusion(bf16[8,288,576]{2,1,0:T(8,128)(2,1)} %bitcast_dynamic-update-slice_fusion, s32[1024]{0:T(1024)S(1)} %pad_clamp_fusion), kind=kCustom, calls=%fused_computation | custom fusion | bytes 5308448 | tf_op jit(solution)/shard_map/gather | solution.py:56
  79.6 4.5 %copy.19 = bf16[288,8,576]{2,1,0:T(8,128)(2,1)} copy(bf16[288,8,576]{2,0,1:T(8,128)(2,1)} %bitcast.34) | data formatting | bytes 5308416 | tf_op jit(solution)/shard_map/transpose | solution.py:11
  84.1 5.6 %reshape.102 = bf16[288,4608]{1,0:T(8,128)(2,1)} reshape(bf16[288,8,576]{2,1,0:T(8,128)(2,1)} %copy.19) | data formatting | bytes 5308416 | tf_op jit(solution)/shard_map/reshape | solution.py:13
  89.7 3.0 reduce-scatter.4.cloned.1.call-done
  92.7 1.1 copy.21
  93.7 4.0 fusion.11
  97.8 0.0 all-reduce.3.cloned.1.call-update
  97.8 0.0 all-gather.3.cloned.1.call-start
  97.8 161.0 %all-reduce.3.cloned.1.call-done = f32[128,4608]{1,0:T(8,128)} async-done(((f32[128,4608]{1,0:T(8,128)}), f32[128,4608]{1,0:T(8,128)}) %all-reduce.3.cloned.1.call-update) | async-done | bytes 2359312 | tf_op jit(solution)/shard_map/psum | solution.py:60
  258.8 2.1 multiply_reduce_fusion.1
  260.9 0.0 copy-start.7
  260.9 0.3 copy-done.1
  261.2 1.4 multiply_reduce_fusion
  262.6 0.0 copy-start.8
  262.6 0.0 copy-start.9
  262.6 1.6 multiply_convert_fusion
  264.2 0.0 all-gather.3.cloned.1.call-update
  264.2 14.7 %all-gather = s32[8,1,128]{2,1,0:T(1,128)S(1)} all-gather(s32[1,1,128]{2,1,0:T(1,128)S(1)} %bitcast.36), channel_id=1, replica_groups=mesh['dp'=8,'tensor'=8,'vocab'=8] {'dp'}, dimensions={0}, use_global_device_ids=true | all-gather | bytes 4608 | tf_op jit(solution)/shard_map/all_gather | solution.py:70
  278.9 0.1 fusion.14
  279.0 45.5 %all-gather.3.cloned.1.call-done = bf16[1024,4608]{1,0:T(8,128)(2,1)} async-done(((bf16[128,4608]{1,0:T(8,128)(2,1)}), bf16[1024,4608]{1,0:T(8,128)(2,1)}) %all-gather.3.cloned.1.call-update) | async-done | bytes 9437200 | tf_op jit(solution)/shard_map/all_gather | solution.py:69
  324.5 6.6 %select_reduce_fusion = (f32[1024]{0:T(1024)S(1)}, f32[1024]{0:T(1024)S(1)}) fusion(s32[1024]{0:T(1024)S(1)} %bitcast.35, s32[256]{0:T(256)S(1)} %iota_add_fusion, bf16[1024,4608]{1,0:T(8,128)(2,1)} %all-gather.3.cloned.1.call-done, bf16[4608,256]{1,0:T(8,128)(2,1)S(1)} %copy-done), kind=kOutput, calls=%fused_computation.17 | convolution fusion | flops 2417752064 | bytes 11809792 | tf_op jit(solution)/shard_map/dot_general | solution.py:74
  331.1 98.1 %all-reduce = (f32[1024]{0:T(1024)S(1)}, f32[1024]{0:T(1024)S(1)}) all-reduce(f32[1024]{0:T(1024)S(1)} %get-tuple-element.6, f32[1024]{0:T(1024)S(1)} %get-tuple-element.5), channel_id=1, replica_groups=mesh['dp'=8,'tensor'=8,'vocab'=8] {'dp','tensor','vocab'}, use_global_device_ids=true, to_apply=%region_9.10 | all-reduce | flops 2048 | bytes 16384 | tf_op jit(solution)/shard_map/psum | solution.py:78
  429.1 0.6 compare_select_fusion.3
  (31 shorter events, 0.1 us)
Async XLA Ops:
  6.5 318.0 %copy-start = (bf16[4608,256]{1,0:T(8,128)(2,1)S(1)}, bf16[4608,256]{1,0:T(8,128)(2,1)}, u32[]{:S(2)}) copy-start(bf16[4608,256]{1,0:T(8,128)(2,1)} %param.17) | copy-start | bytes 7077892
  11.3 37.2 %all-to-all-start = ((bf16[128,8,576]{0,2,1:T(8,128)(2,1)}), bf16[128,8,576]{0,2,1:T(8,128)(2,1)S(1)}, u32[]{:S(2)}, u32[]{:S(2)}) async-start(bf16[128,8,576]{0,2,1:T(8,128)(2,1)} %bitcast.2), calls=%async_computation | async-start | bytes 2359296 | tf_op jit(solution)/shard_map/all_to_all | solution.py:31
  21.7 71.0 %reduce-scatter.4.cloned.1.call-start = ((), (), s32[]{:S(2)}) async-start(), calls=%async_computation.4 | async-start | bytes 1474560
  21.7 17.5 %collective-permute-start = (bf16[288,576]{1,0:T(8,128)(2,1)}, bf16[288,576]{1,0:T(8,128)(2,1)S(1)}, u32[]{:S(2)}, u32[]{:S(2)}) collective-permute-start(bf16[288,576]{1,0:T(8,128)(2,1)} %param.14), channel_id=1, source_target_pairs={{0,64},{64,128},{128,192},{192,256},{256,320},{320,384},{384,448},... | collective-permute-start | bytes 995336 | tf_op jit(solution)/shard_map/ppermute | solution.py:49
  39.1 6.8 %copy-start.4 = (bf16[288,576]{1,0:T(8,128)(2,1)}, bf16[288,576]{1,0:T(8,128)(2,1)S(1)}, u32[]{:S(2)}) copy-start(bf16[288,576]{1,0:T(8,128)(2,1)S(1)} %collective-permute-done) | copy-start | bytes 995332
  39.1 6.8 %collective-permute-start.1 = (bf16[288,576]{1,0:T(8,128)(2,1)S(1)}, bf16[288,576]{1,0:T(8,128)(2,1)}, u32[]{:S(2)}, u32[]{:S(2)}) collective-permute-start(bf16[288,576]{1,0:T(8,128)(2,1)S(1)} %collective-permute-done), channel_id=1, source_target_pairs={{0,64},{64,128},{128,192},{192,256},{256,320},{320,384},{384,448},... | collective-permute-start | bytes 995336 | tf_op jit(solution)/shard_map/ppermute | solution.py:49
  41.5 12.8 %collective-permute-start.4 = (bf16[288,576]{1,0:T(8,128)(2,1)}, bf16[288,576]{1,0:T(8,128)(2,1)}, u32[]{:S(2)}, u32[]{:S(2)}) collective-permute-start(bf16[288,576]{1,0:T(8,128)(2,1)} %param.14), channel_id=1, source_target_pairs={{64,0},{128,64},{192,128},{256,192},{320,256},{384,320},{448,384},... | collective-permute-start | bytes 995336 | tf_op jit(solution)/shard_map/ppermute | solution.py:52
  45.9 10.8 %collective-permute-start.2 = (bf16[288,576]{1,0:T(8,128)(2,1)}, bf16[288,576]{1,0:T(8,128)(2,1)}, u32[]{:S(2)}, u32[]{:S(2)}) collective-permute-start(bf16[288,576]{1,0:T(8,128)(2,1)} %collective-permute-done.1), channel_id=1, source_target_pairs={{0,64},{64,128},{128,192},{192,256},{256,320},{320,384},{384,448},... | collective-permute-start | bytes 995336 | tf_op jit(solution)/shard_map/ppermute | solution.py:49
  54.2 16.1 %copy-start.5 = (bf16[288,576]{1,0:T(8,128)(2,1)S(1)}, bf16[288,576]{1,0:T(8,128)(2,1)}, u32[]{:S(2)}) copy-start(bf16[288,576]{1,0:T(8,128)(2,1)} %copy-done.4) | copy-start | bytes 995332
  54.2 16.9 %copy-start.3 = (bf16[288,576]{1,0:T(8,128)(2,1)S(1)}, bf16[288,576]{1,0:T(8,128)(2,1)}, u32[]{:S(2)}) copy-start(bf16[288,576]{1,0:T(8,128)(2,1)} %param.14) | copy-start | bytes 995332
  54.2 204.6 %all-reduce.3.cloned.1.call-start = ((), (), s32[]{:S(2)}) async-start(), calls=%async_computation.2 | async-start | bytes 4718592 | tf_op jit(solution)/shard_map/psum | solution.py:60
  54.2 7.2 %collective-permute-start.5 = (bf16[288,576]{1,0:T(8,128)(2,1)}, bf16[288,576]{1,0:T(8,128)(2,1)S(1)}, u32[]{:S(2)}, u32[]{:S(2)}) collective-permute-start(bf16[288,576]{1,0:T(8,128)(2,1)} %collective-permute-done.4), channel_id=1, source_target_pairs={{64,0},{128,64},{192,128},{256,192},{320,256},{384,320},{448,384},... | collective-permute-start | bytes 995336 | tf_op jit(solution)/shard_map/ppermute | solution.py:52
  56.7 8.3 %collective-permute-start.3 = (bf16[288,576]{1,0:T(8,128)(2,1)}, bf16[288,576]{1,0:T(8,128)(2,1)}, u32[]{:S(2)}, u32[]{:S(2)}) collective-permute-start(bf16[288,576]{1,0:T(8,128)(2,1)} %collective-permute-done.2), channel_id=1, source_target_pairs={{0,64},{64,128},{128,192},{192,256},{256,320},{320,384},{384,448},... | collective-permute-start | bytes 995336 | tf_op jit(solution)/shard_map/ppermute | solution.py:49
  61.4 13.0 %collective-permute-start.6 = (bf16[288,576]{1,0:T(8,128)(2,1)S(1)}, bf16[288,576]{1,0:T(8,128)(2,1)S(1)}, u32[]{:S(2)}, u32[]{:S(2)}) collective-permute-start(bf16[288,576]{1,0:T(8,128)(2,1)S(1)} %collective-permute-done.5), channel_id=1, source_target_pairs={{64,0},{128,64},{192,128},{256,192},{320,256},{384,320},{448,384},... | collective-permute-start | bytes 995336 | tf_op jit(solution)/shard_map/ppermute | solution.py:52
  97.8 163.1 %copy-start.2 = (bf16[128,4608]{1,0:T(8,128)(2,1)S(1)}, bf16[128,4608]{1,0:T(8,128)(2,1)}, u32[]{:S(2)}) copy-start(bf16[128,4608]{1,0:T(8,128)(2,1)} %param.10) | copy-start | bytes 3538948
  97.8 226.7 %all-gather.3.cloned.1.call-start = ((), (), s32[]{:S(2)}) async-start(), calls=%async_computation.3 | async-start | bytes 10616832 | tf_op jit(solution)/shard_map/all_gather | solution.py:69
  258.8 2.4 copy-start.1
  260.8 1.7 copy-start.6
  260.9 1.7 copy-start.7
  262.6 1.7 copy-start.8
  262.6 16.4 %copy-start.9 = (s32[2]{0:T(128)S(1)}, s32[2]{0:T(128)}, u32[]{:S(2)}) copy-start(s32[2]{0:T(128)} %param.19) | copy-start | bytes 28
Sparse Core Ops, SparseCore 0:
  54.3 38.3 reduce-scatter.3
  97.9 160.8 all-reduce.2
  264.3 60.1 all-gather.2
